TPU v7x, 32 devices: a whole 2x2x4 slice. The times are simulated.
32 devices in a mesh: seg: 4 (over y, x), pen: 8 (over z, core).
Axes of the slice: x: 2, y: 2, z: 4, core: 2. Of those that a mesh axis runs over, the one named last changes fastest.
Arguments:
- state: float32 [16, 384, 384], P('seg', 'pen'), may hold values from -6 to 6
- krylov: float32 [16, 16, 384, 384], P(None, 'seg', 'pen'), may hold values from -15 to 15
Outputs:
- residual: float32 [16, 384, 384], P('seg', 'pen')
- next_vector: float32 [16, 384, 384], P('seg', 'pen')
- hessenberg: float32 [17], replicated
All inputs are finite; a program needn't handle non-finite values.
Results may differ from a plain program's by a relative error of at most 0.0003.
Values sent between devices are 32-bit elements; how exact they have to be, the bound alone decides.
A program may use at most 64 MiB of HBM per device.

v0:
```python
import math

import jax
import jax.numpy as jnp
from jax import lax
from jax.sharding import PartitionSpec as P

NX = 384
NZ = 384
PLANES = 4
STEPS = 2
KRY = 16


time_step = 0.0003
viscosity = 0.0226


def shifted(block, axis, distance):
    devices = range(lax.axis_size(axis))
    route = [((i - distance) % len(devices), i) for i in devices]
    return lax.ppermute(block, axis, route)


def product(formula, former, latter):
    return jnp.einsum(
        formula, former, latter, precision=lax.Precision.HIGHEST, preferred_element_type=jnp.float32
    )


def tables(count):
    indices = jnp.arange(count, dtype=jnp.int32)
    phases = indices[:, None] * indices[None, :] % count
    angles = phases.astype(jnp.float32) * (2.0 * math.pi / count)
    cosines = jnp.cos(angles)
    sines = jnp.sin(angles)
    signed = jnp.where(indices <= count // 2, indices, indices - count).astype(jnp.float32)
    slopes = jnp.where(indices == count // 2, 0.0, signed)
    return (cosines + sines, slopes[:, None] * (cosines - sines), signed)


def tendency(z_slope, z_plain):
    stream_z = z_slope[0:2]
    vortex_z = z_slope[2:4]
    stream_x = z_plain[0:2]
    vortex_x = z_plain[2:4]
    base_term = stream_x[0] * vortex_z[0] - stream_z[0] * vortex_x[0]
    tangent_term = (
        stream_x[1] * vortex_z[0]
        + stream_x[0] * vortex_z[1]
        - stream_z[1] * vortex_x[0]
        - stream_z[0] * vortex_x[1]
    )
    return jnp.stack([base_term, tangent_term])


def advance(fields, inverse_k, damping, basis_x, slopes_x, basis_z, slopes_z, forward_x, forward_z):
    spectra = jnp.concatenate([fields * inverse_k, fields], 0)
    values_x = product("arzx,xj->arzj", spectra, basis_x)
    slopes_along = product("arzx,xj->arzj", spectra, slopes_x)
    z_slope = product(
        "arzx,zj->arxj",
        lax.all_to_all(values_x, "pen", split_axis=3, concat_axis=2, tiled=True),
        slopes_z,
    )
    z_plain = product(
        "arzx,zj->arxj",
        lax.all_to_all(slopes_along, "pen", split_axis=3, concat_axis=2, tiled=True),
        basis_z,
    )
    modes_z = product("arxz,zk->arxk", tendency(z_slope, z_plain), forward_z)
    returned = lax.all_to_all(modes_z, "pen", split_axis=3, concat_axis=2, tiled=True)
    forcing = product("arxz,xk->arzk", returned, forward_x)
    return (fields + time_step * forcing) * damping


def body(state, krylov):
    rank = lax.axis_index("pen")
    zcut = state.shape[1]
    basis_x, slopes_x, signed_x = tables(NX)
    basis_z, slopes_z, signed_z = tables(NZ)
    local_z = lax.dynamic_slice_in_dim(signed_z, rank * zcut, zcut)
    ksquare = local_z[:, None] ** 2 + signed_x[None, :] ** 2
    inverse_k = jnp.where(ksquare > 0, 1.0 / jnp.where(ksquare > 0, ksquare, 1.0), 0.0)
    damping = 1.0 / (1.0 + time_step * viscosity * ksquare)
    forward_x = basis_x / NX
    forward_z = basis_z / NZ
    direction = krylov[KRY - 1]
    fields = jnp.stack([state, direction])
    for repeat in range(STEPS):
        fields = advance(
            fields, inverse_k, damping, basis_x, slopes_x, basis_z, slopes_z, forward_x, forward_z
        )
    moved = shifted(fields, "seg", 1)
    residual = moved[0] - state
    image = moved[1] - direction
    total = float(lax.axis_size("seg") * PLANES * NZ * NX)
    local_dots = product("krzx,rzx->k", krylov, image)
    gram_local = product("krzx,jrzx->kj", krylov, krylov)
    summed, energy, gram = lax.psum(
        (local_dots, jnp.sum(image * image), gram_local), ("seg", "pen")
    )
    coeffs = summed / total
    quadratic = jnp.dot(
        coeffs,
        jnp.dot(gram, coeffs, precision=lax.Precision.HIGHEST),
        precision=lax.Precision.HIGHEST,
    )
    squared = energy - 2.0 * jnp.dot(coeffs, summed, precision=lax.Precision.HIGHEST) + quadratic
    remain = image - product("k,krzx->rzx", coeffs, krylov)
    norm_value = jnp.sqrt(squared / total + 1e-06)
    return (residual, remain / norm_value, jnp.concatenate([coeffs, norm_value[None]]))


def solution(mesh):
    return jax.shard_map(
        body,
        mesh=mesh,
        in_specs=(P("seg", "pen", None), P(None, "seg", "pen", None)),
        out_specs=(P("seg", "pen", None), P("seg", "pen", None), P()),
        check_vma=False,
    )
```

profile of v0, /device:TPU:0, one launch (start us, length us, event | category | flops | bytes accessed | tf_op | source)
XLA Modules:
  0.0 362.6 jit_solution(12359839424391119904)
XLA Ops:
  0.7 1.0 slice.89
  2.5 1.0 fusion.54
  4.4 5.7 %fusion.19 = f32[4,4,48,384]{3,2,1,0:T(8,128)} fusion(f32[1,4,48,384]{3,2,1,0:T(8,128)S(1)} %slice.89, f32[1,4,48,384]{3,2,1,0:T(8,128)S(1)} %bitcast.162, f32[2,4,48,384]{3,2,1,0:T(8,128)S(1)} %fusion.54), kind=kOutput, calls=%fused_computation.27 | convolution fusion | flops 1361018880 | bytes 2359296 | tf_op jit(solution)/shard_map/arzx,xj->arzj/dot_general | solution.py:26
  10.1 3.2 copy.13
  13.3 4.4 %reshape.107 = f32[8,1,36864]{2,1,0:T(1,128)} reshape(f32[384,4,4,48]{3,2,1,0:T(4,128)S(1)} %bitcast.151) | data formatting | bytes 2359296
  17.8 6.7 %all-to-all-start.1 = ((f32[8,1,36864]{2,1,0:T(1,128)}), f32[8,1,36864]{2,1,0:T(1,128)}, u32[]{:S(2)}, u32[]{:S(2)}) async-start(f32[8,1,36864]{2,1,0:T(1,128)} %reshape.107), calls=%async_computation.1 | async-start | bytes 2359296 | tf_op jit(solution)/shard_map/all_to_all | solution.py:63
  24.5 5.8 %fusion.20 = f32[4,4,48,384]{3,2,1,0:T(8,128)} fusion(f32[1,4,48,384]{3,2,1,0:T(8,128)S(1)} %copy-done.2, f32[1,4,48,384]{3,2,1,0:T(8,128)S(1)} %bitcast.163, f32[2,4,48,384]{3,2,1,0:T(8,128)S(1)} %copy-done.7, f32[384]{0:T(512)S(1)} %fusion.86), kind=kOutput, calls=%fused_computation.28 | convolution fusion | flops 1361166336 | bytes 2360832 | tf_op jit(solution)/shard_map/arzx,xj->arzj/dot_general | solution.py:26
  30.3 3.2 copy.11
  33.6 4.4 %reshape.105 = f32[8,1,36864]{2,1,0:T(1,128)} reshape(f32[384,4,4,48]{3,2,1,0:T(4,128)S(1)} %bitcast.152) | data formatting | bytes 2359296
  38.0 15.9 %all-to-all-done.1 = f32[8,1,36864]{2,1,0:T(1,128)} async-done(((f32[8,1,36864]{2,1,0:T(1,128)}), f32[8,1,36864]{2,1,0:T(1,128)}, u32[]{:S(2)}, u32[]{:S(2)}) %all-to-all-start.1) | async-done | bytes 1179680 | tf_op jit(solution)/shard_map/all_to_all | solution.py:63
  53.9 4.5 %all-to-all-start = ((f32[8,1,36864]{2,1,0:T(1,128)}), f32[8,1,36864]{2,1,0:T(1,128)}, u32[]{:S(2)}, u32[]{:S(2)}) async-start(f32[8,1,36864]{2,1,0:T(1,128)} %reshape.105), calls=%async_computation | async-start | bytes 2359296 | tf_op jit(solution)/shard_map/all_to_all | solution.py:68
  59.0 5.7 %reduce.5 = f32[8,36864]{1,0:T(8,128)} reduce(f32[8,1,36864]{2,1,0:T(1,128)} %all-to-all-done.1, f32[]{:T(128)} %broadcast.210), dimensions={1}, to_apply=%all_to_all.82.reduce_sub_computation | reduce | bytes 2359300 | tf_op jit(solution)/shard_map/all_to_all | solution.py:63
  64.7 4.2 %reshape.108 = f32[384,4,4,48]{3,2,1,0:T(4,128)S(1)} reshape(f32[8,36864]{1,0:T(8,128)} %reduce.5) | data formatting | bytes 2359296
  69.0 3.5 copy.57
  72.4 3.3 all_to_all.85
  75.7 5.8 %fusion.38 = f32[4,4,48,384]{3,2,1,0:T(8,128)} fusion(f32[4,4,384,48]{2,3,1,0:T(8,128)S(1)} %all_to_all.85, f32[384]{0:T(512)S(1)} %fusion.86), kind=kOutput, calls=%fused_computation.47 | convolution fusion | flops 1360576512 | bytes 2360832 | tf_op jit(solution)/shard_map/arzx,zj->arxj/dot_general | solution.py:26
  81.5 6.3 %all-to-all-done = f32[8,1,36864]{2,1,0:T(1,128)} async-done(((f32[8,1,36864]{2,1,0:T(1,128)}), f32[8,1,36864]{2,1,0:T(1,128)}, u32[]{:S(2)}, u32[]{:S(2)}) %all-to-all-start) | async-done | bytes 1179680 | tf_op jit(solution)/shard_map/all_to_all | solution.py:68
  87.8 5.7 %reduce.4 = f32[8,36864]{1,0:T(8,128)} reduce(f32[8,1,36864]{2,1,0:T(1,128)} %all-to-all-done, f32[]{:T(128)} %broadcast.210), dimensions={1}, to_apply=%all_to_all.78.reduce_sub_computation | reduce | bytes 2359300 | tf_op jit(solution)/shard_map/all_to_all | solution.py:68
  93.6 4.2 %reshape.106 = f32[384,4,4,48]{3,2,1,0:T(4,128)S(1)} reshape(f32[8,36864]{1,0:T(8,128)} %reduce.4) | data formatting | bytes 2359296
  97.8 3.7 %copy.58 = f32[4,4,48,8,48]{2,3,4,1,0:T(8,128)} copy(f32[4,4,48,8,48]{2,1,0,4,3:T(4,128)S(1)} %bitcast.145) | data formatting | bytes 2359296 | tf_op jit(solution)/shard_map/all_to_all | solution.py:68
  101.5 2.8 all_to_all.81
  104.3 4.7 %fusion.45 = f32[4,4,48,384]{3,2,1,0:T(8,128)S(1)} fusion(f32[4,4,384,48]{2,3,1,0:T(8,128)S(1)} %all_to_all.81), kind=kOutput, calls=%fused_computation.54 | convolution fusion | flops 1360429056 | bytes 2359296 | tf_op jit(solution)/shard_map/arzx,zj->arxj/dot_general | solution.py:26
  109.1 3.7 %fusion.23 = f32[2,4,48,384]{3,2,1,0:T(8,128)S(1)} fusion(f32[1,4,48,384]{3,2,1,0:T(8,128)S(1)} %get-tuple-element.9, f32[1,4,48,384]{3,2,1,0:T(8,128)S(1)} %get-tuple-element.8), kind=kOutput, calls=%fused_computation.32 | convolution fusion | flops 681246720 | bytes 1179648 | tf_op jit(solution)/shard_map/arxz,zk->arxk/dot_general | solution.py:26
  113.6 1.8 reshape.109
  115.5 19.1 %all_to_all.108 = f32[8,1,18432]{2,1,0:T(1,128)S(1)} all-to-all(f32[8,1,18432]{2,1,0:T(1,128)S(1)} %reshape.109), channel_id=1, replica_groups=mesh['seg'=4,'pen'=8] {'pen'}, dimensions={0} | all-to-all | bytes 1179648 | tf_op jit(solution)/shard_map/all_to_all | solution.py:72
  134.6 2.0 reduce.6
  136.6 1.7 reshape.110
  138.4 0.9 copy.60
  140.3 3.7 %broadcast_multiply_fusion = (f32[2,4,48,384]{3,2,1,0:T(8,128)S(1)}, f32[2,4,48,384]{3,2,1,0:T(8,128)S(1)}) fusion(f32[48,384]{1,0:T(8,128)S(1)} %get-tuple-element.13, f32[48,384]{1,0:T(8,128)S(1)} %copy-done.8, f32[2,4,384,48]{2,3,1,0:T(8,128)S(1)} %all_to_all.89, f32[1,4,48,384]{3,2,1,0:T(8,128)S(1)} %copy-done.3, f32[1,4,48,384]{3,2,1,0:T(8,128)S(1)} %bitcast.164), kind=kOutput, calls=%fused_computation.98 | convolution fusion | flops 681836544 | bytes 2506752 | tf_op jit(solution)/shard_map/arxz,xk->arzk/dot_general | solution.py:26
  144.9 6.2 %fusion.17 = f32[4,4,48,384]{3,2,1,0:T(8,128)} fusion(f32[2,4,48,384]{3,2,1,0:T(8,128)S(1)} %get-tuple-element.17, f32[2,4,48,384]{3,2,1,0:T(8,128)S(1)} %get-tuple-element.16), kind=kOutput, calls=%fused_computation.24 | convolution fusion | flops 1360723968 | bytes 2359296 | tf_op jit(solution)/shard_map/arzx,xj->arzj/dot_general | solution.py:26
  151.1 3.2 copy.19
  154.3 4.4 %reshape.113 = f32[8,1,36864]{2,1,0:T(1,128)} reshape(f32[384,4,4,48]{3,2,1,0:T(4,128)S(1)} %bitcast.153) | data formatting | bytes 2359296
  158.8 4.4 %all-to-all-start.4 = ((f32[8,1,36864]{2,1,0:T(1,128)}), f32[8,1,36864]{2,1,0:T(1,128)}, u32[]{:S(2)}, u32[]{:S(2)}) async-start(f32[8,1,36864]{2,1,0:T(1,128)} %reshape.113), calls=%async_computation.4 | async-start | bytes 2359296 | tf_op jit(solution)/shard_map/all_to_all | solution.py:63
  163.2 5.8 %fusion.18 = f32[4,4,48,384]{3,2,1,0:T(8,128)} fusion(f32[2,4,48,384]{3,2,1,0:T(8,128)S(1)} %copy-done.11, f32[2,4,48,384]{3,2,1,0:T(8,128)S(1)} %copy-done.14, f32[384]{0:T(512)S(1)} %fusion.86), kind=kOutput, calls=%fused_computation.25 | convolution fusion | flops 1360871424 | bytes 2360832 | tf_op jit(solution)/shard_map/arzx,xj->arzj/dot_general | solution.py:26
  169.0 3.2 copy.17
  172.3 4.4 %reshape.111 = f32[8,1,36864]{2,1,0:T(1,128)} reshape(f32[384,4,4,48]{3,2,1,0:T(4,128)S(1)} %bitcast.154) | data formatting | bytes 2359296
  176.7 15.9 %all-to-all-done.4 = f32[8,1,36864]{2,1,0:T(1,128)} async-done(((f32[8,1,36864]{2,1,0:T(1,128)}), f32[8,1,36864]{2,1,0:T(1,128)}, u32[]{:S(2)}, u32[]{:S(2)}) %all-to-all-start.4) | async-done | bytes 1179680 | tf_op jit(solution)/shard_map/all_to_all | solution.py:63
  192.6 4.4 %all-to-all-start.3 = ((f32[8,1,36864]{2,1,0:T(1,128)}), f32[8,1,36864]{2,1,0:T(1,128)}, u32[]{:S(2)}, u32[]{:S(2)}) async-start(f32[8,1,36864]{2,1,0:T(1,128)} %reshape.111), calls=%async_computation.3 | async-start | bytes 2359296 | tf_op jit(solution)/shard_map/all_to_all | solution.py:68
  197.0 5.8 %reduce.8 = f32[8,36864]{1,0:T(8,128)} reduce(f32[8,1,36864]{2,1,0:T(1,128)} %all-to-all-done.4, f32[]{:T(128)} %broadcast.210), dimensions={1}, to_apply=%all_to_all.94.reduce_sub_computation | reduce | bytes 2359300 | tf_op jit(solution)/shard_map/all_to_all | solution.py:63
  202.8 4.2 %reshape.114 = f32[384,4,4,48]{3,2,1,0:T(4,128)S(1)} reshape(f32[8,36864]{1,0:T(8,128)} %reduce.8) | data formatting | bytes 2359296
  207.0 3.5 copy.55
  210.5 3.0 all_to_all.97
  213.5 5.8 %fusion.35 = f32[4,4,48,384]{3,2,1,0:T(8,128)} fusion(f32[4,4,384,48]{2,3,1,0:T(8,128)S(1)} %all_to_all.97, f32[384]{0:T(512)S(1)} %fusion.86), kind=kOutput, calls=%fused_computation.44 | convolution fusion | flops 1360576512 | bytes 2360832 | tf_op jit(solution)/shard_map/arzx,zj->arxj/dot_general | solution.py:26
  219.3 7.1 %all-to-all-done.3 = f32[8,1,36864]{2,1,0:T(1,128)} async-done(((f32[8,1,36864]{2,1,0:T(1,128)}), f32[8,1,36864]{2,1,0:T(1,128)}, u32[]{:S(2)}, u32[]{:S(2)}) %all-to-all-start.3) | async-done | bytes 1179680 | tf_op jit(solution)/shard_map/all_to_all | solution.py:68
  226.4 5.7 %reduce.7 = f32[8,36864]{1,0:T(8,128)} reduce(f32[8,1,36864]{2,1,0:T(1,128)} %all-to-all-done.3, f32[]{:T(128)} %broadcast.210), dimensions={1}, to_apply=%all_to_all.90.reduce_sub_computation | reduce | bytes 2359300 | tf_op jit(solution)/shard_map/all_to_all | solution.py:68
  232.1 4.2 %reshape.112 = f32[384,4,4,48]{3,2,1,0:T(4,128)S(1)} reshape(f32[8,36864]{1,0:T(8,128)} %reduce.7) | data formatting | bytes 2359296
  236.4 3.9 %copy.56 = f32[4,4,48,8,48]{2,3,4,1,0:T(8,128)} copy(f32[4,4,48,8,48]{2,1,0,4,3:T(4,128)S(1)} %bitcast.149) | data formatting | bytes 2359296 | tf_op jit(solution)/shard_map/all_to_all | solution.py:68
  240.3 2.8 all_to_all.93
  243.1 4.7 %fusion.42 = f32[4,4,48,384]{3,2,1,0:T(8,128)S(1)} fusion(f32[4,4,384,48]{2,3,1,0:T(8,128)S(1)} %all_to_all.93), kind=kOutput, calls=%fused_computation.51 | convolution fusion | flops 1360429056 | bytes 2359296 | tf_op jit(solution)/shard_map/arzx,zj->arxj/dot_general | solution.py:26
  247.9 3.7 %fusion.27 = f32[2,4,48,384]{3,2,1,0:T(8,128)S(1)} fusion(f32[1,4,48,384]{3,2,1,0:T(8,128)S(1)} %get-tuple-element.7, f32[1,4,48,384]{3,2,1,0:T(8,128)S(1)} %get-tuple-element.6), kind=kOutput, calls=%fused_computation.36 | convolution fusion | flops 681246720 | bytes 1179648 | tf_op jit(solution)/shard_map/arxz,zk->arxk/dot_general | solution.py:26
  252.4 1.8 reshape.115
  254.2 19.3 %all_to_all.109 = f32[8,1,18432]{2,1,0:T(1,128)S(1)} all-to-all(f32[8,1,18432]{2,1,0:T(1,128)S(1)} %reshape.115), channel_id=1, replica_groups=mesh['seg'=4,'pen'=8] {'pen'}, dimensions={0} | all-to-all | bytes 1179648 | tf_op jit(solution)/shard_map/all_to_all | solution.py:72
  273.6 2.0 reduce.9
  275.6 1.7 reshape.116
  277.3 2.1 copy.59
  279.4 2.0 all_to_all.101
  281.5 3.7 %fusion.9 = f32[2,4,48,384]{3,2,1,0:T(8,128)S(1)} fusion(f32[2,4,48,384]{3,2,1,0:T(8,128)S(1)} %copy-done.12, f32[2,4,384,48]{2,3,1,0:T(8,128)S(1)} %all_to_all.101, f32[48,384]{1,0:T(8,128)S(1)} %copy-done.9), kind=kOutput, calls=%fused_computation.17 | convolution fusion | flops 681541632 | bytes 1843200 | tf_op jit(solution)/shard_map/arxz,xk->arzk/dot_general | solution.py:26
  285.1 1.8 collective-permute-start
  286.9 14.2 %fusion.10 = f32[16,16]{1,0:T(8,128)S(1)} fusion(f32[16,4,48,384]{3,2,1,0:T(8,128)} %param.3), kind=kOutput, calls=%fused_computation.20 | convolution fusion | flops 226492416 | bytes 4719616 | tf_op jit(solution)/shard_map/krzx,jrzx->kj/dot_general | solution.py:26
  301.3 1.0 fusion.136
  302.3 7.9 %fusion.13 = f32[16]{0:T(128)S(1)} fusion(f32[16,4,48,384]{3,2,1,0:T(8,128)S(1)} %bitcast.142, f32[4,48,384,1]{2,1,0,3:T(8,128)S(1)} %fusion.136), kind=kOutput, calls=%fused_computation.21 | convolution fusion | flops 14155776 | bytes 5013568 | tf_op jit(solution)/shard_map/krzx,rzx->k/dot_general | solution.py:26
  311.0 38.3 %all-reduce = (f32[16]{0:T(128)S(1)}, f32[]{:T(128)}, f32[16,16]{1,0:T(8,128)S(1)}) all-reduce(f32[16]{0:T(128)S(1)} %fusion.13, f32[]{:T(128)} %fusion.67, f32[16,16]{1,0:T(8,128)S(1)} %fusion.10), channel_id=1, replica_groups=mesh['seg'=4,'pen'=8] {'seg','pen'}, use_global_device_ids=true, to_apply=%region_0.1 | all-reduce | flops 273 | bytes 2184 | tf_op jit(solution)/shard_map/psum | solution.py:100
  349.9 7.2 %fusion.2 = f32[1,4,48,384]{3,0,2,1:T(1,128)S(1)} fusion(f32[16,4,48,384]{3,2,1,0:T(8,128)} %param.3, f32[16]{0:T(128)S(1)} %get-tuple-element.3), kind=kOutput, calls=%fused_computation.2 | convolution fusion | flops 14155792 | bytes 5013568 | tf_op jit(solution)/shard_map/k,krzx->rzx/dot_general | solution.py:26
  360.4 1.8 fusion.66
  (51 shorter events, 8.9 us)
Async XLA Ops:
  0.6 3.7 %copy-start = (f32[4,48,384]{2,1,0:T(8,128)S(1)}, f32[4,48,384]{2,1,0:T(8,128)}, u32[]{:S(2)}) copy-start(f32[4,48,384]{2,1,0:T(8,128)} %param.2) | copy-start | bytes 884740
  1.7 1.8 copy-start.1
  3.5 0.8 copy-start.6
  17.8 6.7 %copy-start.2 = (f32[1,4,48,384]{3,2,1,0:T(8,128)S(1)}, f32[1,4,48,384]{3,2,1,0:T(8,128)}, u32[]{:S(2)}) copy-start(f32[1,4,48,384]{3,2,1,0:T(8,128)} %copy-done.1) | copy-start | bytes 884740
  17.8 6.8 %copy-start.7 = (f32[2,4,48,384]{3,2,1,0:T(8,128)S(1)}, f32[2,4,48,384]{3,2,1,0:T(8,128)}, u32[]{:S(2)}) copy-start(f32[2,4,48,384]{3,2,1,0:T(8,128)} %copy-done.6) | copy-start | bytes 1769476
  17.8 36.2 %all-to-all-start.1 = ((f32[8,1,36864]{2,1,0:T(1,128)}), f32[8,1,36864]{2,1,0:T(1,128)}, u32[]{:S(2)}, u32[]{:S(2)}) async-start(f32[8,1,36864]{2,1,0:T(1,128)} %reshape.107), calls=%async_computation.1 | async-start | bytes 2359296 | tf_op jit(solution)/shard_map/all_to_all | solution.py:63
  53.9 33.9 %all-to-all-start = ((f32[8,1,36864]{2,1,0:T(1,128)}), f32[8,1,36864]{2,1,0:T(1,128)}, u32[]{:S(2)}, u32[]{:S(2)}) async-start(f32[8,1,36864]{2,1,0:T(1,128)} %reshape.105), calls=%async_computation | async-start | bytes 2359296 | tf_op jit(solution)/shard_map/all_to_all | solution.py:68
  104.3 4.7 %copy-start.5 = (f32[4,4,48,384]{3,2,1,0:T(8,128)S(1)}, f32[4,4,48,384]{3,2,1,0:T(8,128)}, u32[]{:S(2)}) copy-start(f32[4,4,48,384]{3,2,1,0:T(8,128)} %fusion.38) | copy-start | bytes 3538948
  139.3 1.0 copy-start.3
  139.3 1.0 copy-start.8
  143.9 0.8 copy-start.10
  144.0 1.0 copy-start.13
  158.8 4.4 %copy-start.11 = (f32[2,4,48,384]{3,2,1,0:T(8,128)S(1)}, f32[2,4,48,384]{3,2,1,0:T(8,128)}, u32[]{:S(2)}) copy-start(f32[2,4,48,384]{3,2,1,0:T(8,128)} %copy-done.10) | copy-start | bytes 1769476
  158.8 4.4 %copy-start.14 = (f32[2,4,48,384]{3,2,1,0:T(8,128)S(1)}, f32[2,4,48,384]{3,2,1,0:T(8,128)}, u32[]{:S(2)}) copy-start(f32[2,4,48,384]{3,2,1,0:T(8,128)} %copy-done.13) | copy-start | bytes 1769476
  158.8 33.8 %all-to-all-start.4 = ((f32[8,1,36864]{2,1,0:T(1,128)}), f32[8,1,36864]{2,1,0:T(1,128)}, u32[]{:S(2)}, u32[]{:S(2)}) async-start(f32[8,1,36864]{2,1,0:T(1,128)} %reshape.113), calls=%async_computation.4 | async-start | bytes 2359296 | tf_op jit(solution)/shard_map/all_to_all | solution.py:63
  192.6 33.8 %all-to-all-start.3 = ((f32[8,1,36864]{2,1,0:T(1,128)}), f32[8,1,36864]{2,1,0:T(1,128)}, u32[]{:S(2)}, u32[]{:S(2)}) async-start(f32[8,1,36864]{2,1,0:T(1,128)} %reshape.111), calls=%async_computation.3 | async-start | bytes 2359296 | tf_op jit(solution)/shard_map/all_to_all | solution.py:68
  243.1 4.7 %copy-start.4 = (f32[4,4,48,384]{3,2,1,0:T(8,128)S(1)}, f32[4,4,48,384]{3,2,1,0:T(8,128)}, u32[]{:S(2)}) copy-start(f32[4,4,48,384]{3,2,1,0:T(8,128)} %fusion.35) | copy-start | bytes 3538948
  277.3 25.0 %slice-start = ((s8[4718592]{0:T(1024)(128)(4,1)}), s8[524288]{0:T(1024)(128)(4,1)S(1)}, s32[]{:S(2)}) async-start(s8[4718592]{0:T(1024)(128)(4,1)} %bitcast.141), calls=%async_computation.6 | async-start | bytes 1048576
  279.4 2.0 copy-start.9
  279.4 2.0 copy-start.12
  281.4 20.9 %slice-start.1 = ((s8[4718592]{0:T(1024)(128)(4,1)}), s8[4194304]{0:T(1024)(128)(4,1)S(1)}, s32[]{:S(2)}) async-start(s8[4718592]{0:T(1024)(128)(4,1)} %bitcast.141), calls=%async_computation.7 | async-start | bytes 8388608
  285.1 16.2 %collective-permute-start = (f32[2,4,48,384]{3,2,1,0:T(8,128)S(1)}, f32[2,4,48,384]{3,2,1,0:T(8,128)S(1)}, u32[]{:S(2)}, u32[]{:S(2)}) collective-permute-start(f32[2,4,48,384]{3,2,1,0:T(8,128)S(1)} %fusion.9), channel_id=1, source_target_pairs={{24,0},{0,8},{8,16},{16,24},{25,1},{1,9},{9,17},{17,25},{26,2},{2,... | collective-permute-start | bytes 1769480 | tf_op jit(solution)/shard_map/ppermute | solution.py:22
where the time goes:
time: 370 us; the launch traced here: 363 us
  local copies, waits for them, and re-layouts  91.9 us (25%)
  matrix products  89.4 us (24%)
  blocking collectives  76.8 us (21%)
  waiting for transfers between devices  45.4 us (12%)
  other arithmetic  33.8 us (9%)
  starting transfers between devices  21.8 us (6%)
    dot_general x15, matrix products, product(): jnp.einsum(formula, former, latter, precision=lax.Precision.HIGHEST, pref...  88.6 us
    unnamed x46, local copies, waits for them, and re-layouts  44 us
    all_to_all x2, blocking collectives, advance(): lax.all_to_all(modes_z, 'pen', split_axis=3, concat_axis=2, tiled=True)  38.5 us
    psum x1, blocking collectives, body(): lax.psum((local_dots, jnp.sum(image * image), gram_local), ('seg', 'pen'))  38.3 us
    all_to_all x2, waiting for transfers between devices, advance(): lax.all_to_all(values_x, 'pen', split_axis=3, concat_axis=2, tiled=True)  31.8 us
    dot_general x6, local copies, waits for them, and re-layouts, product(): jnp.einsum(formula, former, latter, precision=lax.Precision.HIGHEST, pref...  14.5 us
    all_to_all x5, local copies, waits for them, and re-layouts, advance(): lax.all_to_all(slopes_along, 'pen', split_axis=3, concat_axis=2, tiled=True)  13.6 us
    all_to_all x2, waiting for transfers between devices, advance(): lax.all_to_all(slopes_along, 'pen', split_axis=3, concat_axis=2, tiled=True)  13.4 us
  transfers between devices with their start and end apart: 5, of which 5 were waited for; matrix products, arithmetic and copies ran while one was open for 22% of the time, Pallas kernels for 0%

commit v1 on v0

--- a/solution.py
+++ b/solution.py
@@ -1,15 +1,17 @@
+import functools
 import math
 
 import jax
 import jax.numpy as jnp
+import ml_dtypes
+import numpy as np
 from jax import lax
+from jax.experimental import pallas as pl
+from jax.experimental.pallas import tpu as pltpu
 from jax.sharding import PartitionSpec as P
 
-NX = 384
-NZ = 384
-PLANES = 4
 STEPS = 2
-KRY = 16
+MESH = pl.DeviceIdType.MESH
 
 
 time_step = 0.0003
@@ -77,15 +79,18 @@
 def body(state, krylov):
     rank = lax.axis_index("pen")
     zcut = state.shape[1]
-    basis_x, slopes_x, signed_x = tables(NX)
-    basis_z, slopes_z, signed_z = tables(NZ)
+    planes = state.shape[0]
+    modes_x = state.shape[2]
+    modes_z = state.shape[1] * lax.axis_size("pen")
+    basis_x, slopes_x, signed_x = tables(state.shape[2])
+    basis_z, slopes_z, signed_z = tables(zcut * lax.axis_size("pen"))
     local_z = lax.dynamic_slice_in_dim(signed_z, rank * zcut, zcut)
     ksquare = local_z[:, None] ** 2 + signed_x[None, :] ** 2
     inverse_k = jnp.where(ksquare > 0, 1.0 / jnp.where(ksquare > 0, ksquare, 1.0), 0.0)
     damping = 1.0 / (1.0 + time_step * viscosity * ksquare)
-    forward_x = basis_x / NX
-    forward_z = basis_z / NZ
-    direction = krylov[KRY - 1]
+    forward_x = basis_x / modes_x
+    forward_z = basis_z / modes_z
+    direction = krylov[-1]
     fields = jnp.stack([state, direction])
     for repeat in range(STEPS):
         fields = advance(
@@ -94,7 +99,7 @@
     moved = shifted(fields, "seg", 1)
     residual = moved[0] - state
     image = moved[1] - direction
-    total = float(lax.axis_size("seg") * PLANES * NZ * NX)
+    total = float(lax.axis_size("seg") * planes * modes_z * modes_x)
     local_dots = product("krzx,rzx->k", krylov, image)
     gram_local = product("krzx,jrzx->kj", krylov, krylov)
     summed, energy, gram = lax.psum(
@@ -112,11 +117,456 @@
     return (residual, remain / norm_value, jnp.concatenate([coeffs, norm_value[None]]))
 
 
+def split(values):
+    high = values.astype(jnp.bfloat16)
+    low = (values - high.astype(jnp.float32)).astype(jnp.bfloat16)
+    return high, low
+
+
+def host_split(values):
+    values = values.astype(np.float32)
+    high = values.astype(ml_dtypes.bfloat16)
+    low = (values - high.astype(np.float32)).astype(ml_dtypes.bfloat16)
+    return high, low
+
+
+def left_table(values):
+    high, low = host_split(values)
+    return np.concatenate([high, low, high], -1)
+
+
+def right_table(values):
+    high, low = host_split(values)
+    return np.concatenate([high, high, low], -2)
+
+
+def host_tables(count):
+    indices = np.arange(count)
+    angles = 2.0 * np.pi * (indices[:, None] * indices[None, :] % count) / count
+    signed = np.where(indices <= count // 2, indices, indices - count).astype(np.float64)
+    slopes = np.where(indices == count // 2, 0.0, signed)
+    cas = np.cos(angles) + np.sin(angles)
+    return cas, np.cos(angles) - np.sin(angles), slopes, signed
+
+
+def constants(modes_z, modes_x):
+    cas_z, turned_z, _, signed_z = host_tables(modes_z)
+    cas_x, turned_x, slopes_x, signed_x = host_tables(modes_x)
+    slope_x = slopes_x[:, None] * turned_x
+    half = modes_z // 2
+    into = [
+        left_table(np.concatenate([cas_z[:half, c::2].T, turned_z[:half, c::2].T], 0))
+        for c in range(2)
+    ]
+    back = [left_table(cas_z[:half, c::2]) for c in range(2)]
+    ksq = signed_z[:, None] ** 2 + signed_x[None, :] ** 2
+    inverse = np.where(ksq > 0, 1.0 / np.where(ksq > 0, ksq, 1.0), 0.0).astype(np.float32)
+    damping = (1.0 / (1.0 + time_step * viscosity * ksq)).astype(np.float32)
+    return (
+        np.stack(into), np.stack(back), right_table(cas_x), right_table(slope_x), inverse, damping
+    )
+
+
+def kernel(
+    segs, pens,
+    state_hbm, krylov_hbm, into_hbm, back_hbm, cas_hbm, slope_hbm, inverse_hbm, damping_hbm,
+    residual_ref, next_ref, hess_ref,
+    stored, start, into_t, back_t, cas_t, slope_t, inverse, damping,
+    field, wide, tall, base, tangent, mine, theirs, ending, arrived, image,
+    accum, pay, gather_pen, gather_seg, spread, pay_n, norm_pen, norm_seg,
+    load_sem, local_sem, in_send, in_recv, fwd_send, swap_send, swap_recv,
+    out_send, out_recv, pen_send, pen_recv, seg_send, seg_recv,
+):
+    seg = lax.axis_index("seg")
+    pen = lax.axis_index("pen")
+    planes, cut, modes_x = stored.shape[1:]
+    kry = stored.shape[0]
+    modes_z = cut * pens
+    half = modes_z // 2
+    chip = pen // 2
+    core = pen % 2
+    sibling = chip * 2 + 1 - core
+    following = lax.rem(seg + 1, segs)
+    preceding = lax.rem(seg + segs - 1, segs)
+
+    def remote(src, dst, send, recv, to_seg, to_pen):
+        return pltpu.make_async_remote_copy(
+            src_ref=src, dst_ref=dst, send_sem=send, recv_sem=recv,
+            device_id=(to_seg, to_pen), device_id_type=MESH,
+        )
+
+    def rows(owner):
+        return pl.ds(pl.multiple_of(owner * cut, cut), cut)
+
+    loads = [
+        pltpu.make_async_copy(src, dst, load_sem.at[i])
+        for i, (src, dst) in enumerate([
+            (inverse_hbm, inverse), (into_hbm.at[core], into_t), (cas_hbm, cas_t),
+            (slope_hbm, slope_t), (back_hbm.at[core], back_t), (damping_hbm, damping),
+            (state_hbm, start), (krylov_hbm, stored),
+        ])
+    ]
+    for load in loads:
+        load.start()
+
+    barrier = pltpu.get_barrier_semaphore()
+
+    def greet(to_seg, to_pen):
+        pl.semaphore_signal(barrier, inc=1, device_id=(to_seg, to_pen), device_id_type=MESH)
+
+    for i in range(1, pens):
+        greet(seg, lax.rem(pen + i, pens))
+    for i in range(planes):
+        greet(following, core * planes + i)
+        greet(preceding, i * 2 + pen // planes)
+    for i in range(1, segs):
+        greet(lax.rem(seg + i, segs), pen)
+    pl.semaphore_wait(barrier, pens - 1 + 2 * planes + segs - 1)
+
+    sources = [lambda plane: state_hbm.at[plane], lambda plane: krylov_hbm.at[kry - 1, plane]]
+    pending = []
+    own = []
+    for f in range(2):
+        for i in range(1, planes):
+            plane = lax.rem(chip + i, planes)
+            copy = remote(
+                sources[f](plane), field.at[f, rows(pen)], in_send.at[f, i], in_recv.at[f, pen],
+                seg, plane * 2 + core,
+            )
+            copy.start()
+            pending.append(copy)
+        copy = remote(
+            sources[f](chip), field.at[f, rows(pen)], in_send.at[f, 0], in_recv.at[f, pen],
+            seg, sibling,
+        )
+        copy.start()
+        pending.append(copy)
+        copy = pltpu.make_async_copy(sources[f](chip), field.at[f, rows(pen)], local_sem.at[f])
+        copy.start()
+        own.append(copy)
+
+    def awaited(f, owner):
+        place = field.at[f, rows(owner)]
+        remote(place, place, in_send.at[f, 0], in_recv.at[f, owner], seg, sibling).wait_recv()
+
+    forwards = [[], []]
+
+    def relay(f):
+        for i in range(1, planes):
+            owner = lax.rem(chip + i, planes) * 2 + core
+            awaited(f, owner)
+            place = field.at[f, rows(owner)]
+            copy = remote(
+                place, place, fwd_send.at[f, i], in_recv.at[f, owner], seg, sibling
+            )
+            copy.start()
+            forwards[f].append(copy)
+
+    def complete(f):
+        own[f].wait()
+        for i in range(planes):
+            awaited(f, lax.rem(chip + i, planes) * 2 + 1 - core)
+
+    sign = (1 - 2 * core).astype(jnp.float32)
+
+    number = lax.broadcasted_iota(jnp.int32, (half, 1), 0)
+    slope_top = number.astype(jnp.float32)
+    slope_low = jnp.where(number == 0, 0, number - half).astype(jnp.float32)
+
+    def derive(f, out):
+        for way, table in ((0, slope_t), (1, cas_t)):
+            for part in range(2):
+                top = field[f, 0:half, :]
+                low = field[f, half:modes_z, :]
+                if part == 0:
+                    top = top * inverse[0:half, :]
+                    low = low * inverse[half:modes_z, :]
+                if way == 1:
+                    top = top * slope_top
+                    low = low * slope_low
+                high, rest = split(top + sign * low)
+                lanes = slice(part * modes_x, (part + 1) * modes_x)
+                wide[0:half, lanes] = high
+                wide[half:modes_z, lanes] = high
+                wide[modes_z:modes_z + half, lanes] = rest
+            mixed = jnp.dot(
+                into_t[way * half:(way + 1) * half, :], wide[...],
+                preferred_element_type=jnp.float32,
+            )
+            for part in range(2):
+                lines = slice(part * half, (part + 1) * half)
+                high, rest = split(mixed[:, part * modes_x:(part + 1) * modes_x])
+                tall[lines, 0:modes_x] = high
+                tall[lines, modes_x:2 * modes_x] = rest
+                tall[lines, 2 * modes_x:3 * modes_x] = high
+            out[way] = jnp.dot(tall[...], table[...], preferred_element_type=jnp.float32)
+
+    def swap(f, step):
+        n = step * 2 + f
+        return remote(
+            mine.at[n], theirs.at[n], swap_send.at[n], swap_recv.at[n], seg, sibling
+        )
+
+    def give_back(f, step, value):
+        high, rest = split(value)
+        lanes = slice(0, modes_x)
+        wide[0:half, lanes] = high
+        wide[half:modes_z, lanes] = high
+        wide[modes_z:modes_z + half, lanes] = rest
+        mixed = jnp.dot(back_t[...], wide[:, lanes], preferred_element_type=jnp.float32)
+        high, rest = split(mixed)
+        lines = slice(0, half)
+        tall[lines, 0:modes_x] = high
+        tall[lines, modes_x:2 * modes_x] = rest
+        tall[lines, 2 * modes_x:3 * modes_x] = high
+        mine[step * 2 + f] = jnp.dot(
+            tall[lines, :], cas_t[...], preferred_element_type=jnp.float32
+        )
+        swap(f, step).start()
+
+    def base_step(step):
+        derive(0, base)
+        upper, lower = slice(0, half), slice(half, modes_z)
+        give_back(0, step, base[0, upper] * base[1, lower] - base[1, upper] * base[0, lower])
+
+    def tangent_step(step):
+        derive(1, tangent)
+        upper, lower = slice(0, half), slice(half, modes_z)
+        give_back(
+            1, step,
+            tangent[0, upper] * base[1, lower] + base[0, upper] * tangent[1, lower]
+            - tangent[1, upper] * base[0, lower] - base[1, upper] * tangent[0, lower],
+        )
+
+    scale = time_step / (modes_z * modes_x)
+
+    def update(f, step):
+        n = step * 2 + f
+        swap(f, step).wait()
+        own_part = mine[n] * scale
+        other = theirs[n] * scale
+        field[f, 0:half, :] = (field[f, 0:half, :] + (own_part + other)) * damping[0:half, :]
+        field[f, half:modes_z, :] = (
+            field[f, half:modes_z, :] + sign * (own_part - other)
+        ) * damping[half:modes_z, :]
+
+    def finish(f):
+        n = (STEPS - 1) * 2 + f
+        swap(f, STEPS - 1).wait()
+        part = pl.ds(pl.multiple_of(core * half, half), half)
+        change = jnp.where(core == 0, mine[n] + theirs[n], theirs[n] - mine[n])
+        ending[f] = (field[f, part, :] + scale * change) * damping[part, :]
+        for i in range(planes):
+            copy = remote(
+                ending.at[f, i * cut:(i + 1) * cut], arrived.at[f, chip],
+                out_send.at[f, i], out_recv.at[f, chip], following, core * planes + i,
+            )
+            copy.start()
+            pending.append(copy)
+
+    relay(0)
+    for load in loads[:5]:
+        load.wait()
+    complete(0)
+    base_step(0)
+    relay(1)
+    complete(1)
+    tangent_step(0)
+    loads[5].wait()
+    for f in range(2):
+        for copy in forwards[f]:
+            copy.wait_send()
+    for step in range(1, STEPS):
+        update(0, step - 1)
+        base_step(step)
+        update(1, step - 1)
+        if step == STEPS - 1:
+            finish(0)
+        tangent_step(step)
+    finish(1)
+    loads[6].wait()
+    loads[7].wait()
+
+    def landed(f, plane):
+        remote(
+            ending.at[f, 0:cut], arrived.at[f, plane], out_send.at[f, 0], out_recv.at[f, plane],
+            following, pen,
+        ).wait_recv()
+
+    for plane in range(planes):
+        landed(0, plane)
+        residual_ref[plane] = arrived[0, plane] - start[plane]
+
+    def fold(values):
+        summed = jnp.sum(values.reshape(cut // 8, 8, modes_x), axis=0)
+        total = summed[:, 0:128]
+        for lane in range(128, modes_x, 128):
+            total = total + summed[:, lane:lane + 128]
+        return total
+
+    for plane in range(planes):
+        landed(1, plane)
+        image[plane] = arrived[1, plane] - stored[kry - 1, plane]
+
+    accum[...] = jnp.zeros_like(accum)
+
+    def dots(plane, _):
+        values = image[plane]
+        for k in range(kry):
+            accum[k] += fold(stored[k, plane] * values)
+        return 0
+
+    lax.fori_loop(0, planes, dots, 0)
+    pay[0] = jnp.sum(accum[...], axis=1)
+
+    def gather(source, over_pen, over_seg, turn):
+        over_pen[pen] = source[0]
+        copies = []
+        for i in range(1, pens):
+            copy = remote(
+                source.at[0], over_pen.at[pen], pen_send.at[turn, i], pen_recv.at[turn, pen],
+                seg, lax.rem(pen + i, pens),
+            )
+            copy.start()
+            copies.append(copy)
+        for i in range(1, pens):
+            owner = lax.rem(pen + i, pens)
+            remote(
+                source.at[0], over_pen.at[owner], pen_send.at[turn, i],
+                pen_recv.at[turn, owner], seg, owner,
+            ).wait_recv()
+        source[1] = jnp.sum(over_pen[...], axis=0)
+        over_seg[seg] = source[1]
+        for i in range(1, segs):
+            copy = remote(
+                source.at[1], over_seg.at[seg], seg_send.at[turn, i], seg_recv.at[turn, seg],
+                lax.rem(seg + i, segs), pen,
+            )
+            copy.start()
+            copies.append(copy)
+        for i in range(1, segs):
+            owner = lax.rem(seg + i, segs)
+            remote(
+                source.at[1], over_seg.at[owner], seg_send.at[turn, i],
+                seg_recv.at[turn, owner], owner, pen,
+            ).wait_recv()
+        pending.extend(copies)
+        return jnp.sum(over_seg[...], axis=0)
+
+    total = float(segs * planes * modes_z * modes_x)
+    coeffs = jnp.sum(gather(pay, gather_pen, gather_seg, 0), axis=1, keepdims=True) / total
+    spread[...] = jnp.broadcast_to(coeffs, spread.shape)
+    hess_ref[0:kry] = spread[...]
+
+    pay_n[0] = jnp.zeros_like(pay_n[0])
+
+    def remains(plane, _):
+        values = image[plane]
+        for k in range(kry):
+            values = values - spread[k:k + 1, 0:1] * stored[k, plane]
+        image[plane] = values
+        pay_n[0] += fold(values * values)
+        return 0
+
+    lax.fori_loop(0, planes, remains, 0)
+    squared = jnp.sum(gather(pay_n, norm_pen, norm_seg, 1), keepdims=True)
+    norm = jnp.sqrt(squared / total + 1e-06)
+    hess_ref[kry:kry + 8] = jnp.broadcast_to(norm, (8, 128))
+    factor = 1.0 / norm
+    for plane in range(planes):
+        next_ref[plane] = image[plane] * factor
+    for copy in pending:
+        copy.wait_send()
+
+
+def fused(state, krylov, *, tables_of, segs, pens):
+    planes, cut, modes_x = state.shape
+    kry = krylov.shape[0]
+    modes_z = cut * pens
+    half = modes_z // 2
+    f32, bf16 = jnp.float32, jnp.bfloat16
+    dma = pltpu.SemaphoreType.DMA
+    vmem = pltpu.VMEM
+    residual, next_vector, hess = pl.pallas_call(
+        functools.partial(kernel, segs, pens),
+        out_shape=(
+            jax.ShapeDtypeStruct(state.shape, f32),
+            jax.ShapeDtypeStruct(state.shape, f32),
+            jax.ShapeDtypeStruct((kry + 8, 128), f32),
+        ),
+        in_specs=[pl.BlockSpec(memory_space=pl.ANY)] * 8,
+        out_specs=(pl.BlockSpec(memory_space=pltpu.VMEM),) * 3,
+        scratch_shapes=[
+            vmem(krylov.shape, f32),
+            vmem(state.shape, f32),
+            vmem((modes_z, 3 * half), bf16),
+            vmem((half, 3 * half), bf16),
+            vmem((3 * modes_x, modes_x), bf16),
+            vmem((3 * modes_x, modes_x), bf16),
+            vmem((modes_z, modes_x), f32),
+            vmem((modes_z, modes_x), f32),
+            vmem((2, modes_z, modes_x), f32),
+            vmem((3 * half, 2 * modes_x), bf16),
+            vmem((modes_z, 3 * modes_x), bf16),
+            vmem((2, modes_z, modes_x), f32),
+            vmem((2, modes_z, modes_x), f32),
+            vmem((2 * STEPS, half, modes_x), f32),
+            vmem((2 * STEPS, half, modes_x), f32),
+            vmem((2, half, modes_x), f32),
+            vmem((2, planes, cut, modes_x), f32),
+            vmem((planes, cut, modes_x), f32),
+            vmem((kry, 8, 128), f32),
+            vmem((2, kry, 128), f32),
+            vmem((pens, kry, 128), f32),
+            vmem((segs, kry, 128), f32),
+            vmem((kry, 128), f32),
+            vmem((2, 8, 128), f32),
+            vmem((pens, 8, 128), f32),
+            vmem((segs, 8, 128), f32),
+            dma((8,)),
+            dma((2,)),
+            dma((2, planes)),
+            dma((2, pens)),
+            dma((2, planes)),
+            dma((2 * STEPS,)),
+            dma((2 * STEPS,)),
+            dma((2, planes)),
+            dma((2, planes)),
+            dma((2, pens)),
+            dma((2, pens)),
+            dma((2, segs)),
+            dma((2, segs)),
+        ],
+        compiler_params=pltpu.CompilerParams(
+            collective_id=0, has_side_effects=True, vmem_limit_bytes=50 * 1024 * 1024
+        ),
+    )(state, krylov, *[jnp.asarray(t) for t in tables_of])
+    return residual, next_vector, hess[:kry + 1, 0]
+
+
 def solution(mesh):
-    return jax.shard_map(
-        body,
-        mesh=mesh,
-        in_specs=(P("seg", "pen", None), P(None, "seg", "pen", None)),
-        out_specs=(P("seg", "pen", None), P("seg", "pen", None), P()),
-        check_vma=False,
-    )
+    segs, pens = mesh.shape["seg"], mesh.shape["pen"]
+
+    def whole(state, krylov):
+        rows, modes_z, modes_x = state.shape
+        planes, cut = rows // segs, modes_z // pens
+        local = body
+        if (
+            pens == 2 * planes
+            and cut % 8 == 0
+            and modes_z % 32 == 0
+            and modes_x % 128 == 0
+            and krylov.shape[0] % 8 == 0
+        ):
+            local = functools.partial(
+                fused, tables_of=constants(modes_z, modes_x), segs=segs, pens=pens
+            )
+        return jax.shard_map(
+            local,
+            mesh=mesh,
+            in_specs=(P("seg", "pen", None), P(None, "seg", "pen", None)),
+            out_specs=(P("seg", "pen", None), P("seg", "pen", None), P()),
+            check_vma=False,
+        )(state, krylov)
+
+    return whole

time: 370 us -> 68.1 us (0.18); the launches traced: 363 us -> 67.8 us
  matrix products: 89.4 us -> 0 us
  local copies, waits for them, and re-layouts: 91.9 us -> 7.33 us
  blocking collectives: 76.8 us -> 0 us
  Pallas kernels: 0 us -> 59.8 us
  waiting for transfers between devices: 45.4 us -> 0 us
  other arithmetic: 33.8 us -> 0 us
  starting transfers between devices: 21.8 us -> 0 us
    dot_general x16 -> x0, matrix products: 89.4 us -> none  [the longest x15 88.6 us: product(): jnp.einsum(formula, former, latter, precision=lax.Precision.HIGHEST, pref...]
    pallas_call x0 -> x1, Pallas kernels: none -> 59.8 us  [fused(): pl.pallas_call(functools.partial(kernel, segs, pens), out_shape=(jax.Shap...]
    all_to_all x4 -> x0, waiting for transfers between devices: 45.2 us -> none  [the longest x2 31.8 us: advance(): lax.all_to_all(values_x, 'pen', split_axis=3, concat_axis=2, tiled=True)]
    all_to_all x2 -> x0, blocking collectives: 38.5 us -> none  [advance(): lax.all_to_all(modes_z, 'pen', split_axis=3, concat_axis=2, tiled=True)]
    psum x1 -> x0, blocking collectives: 38.3 us -> none  [body(): lax.psum((local_dots, jnp.sum(image * image), gram_local), ('seg', 'pen'))]
    unnamed x46 -> x12, local copies, waits for them, and re-layouts: 44 us -> 6.71 us
    all_to_all x13 -> x0, local copies, waits for them, and re-layouts: 32.3 us -> none  [the longest x5 13.6 us: advance(): lax.all_to_all(slopes_along, 'pen', split_axis=3, concat_axis=2, tiled=True)]
    all_to_all x6 -> x0, other arithmetic: 27 us -> none  [the longest x2 11.5 us: advance(): lax.all_to_all(values_x, 'pen', split_axis=3, concat_axis=2, tiled=True)]
  transfers between devices with their start and end apart: 5 -> 0, of which waited for: 5 -> 0; matrix products, arithmetic and copies ran while one was open for 22% -> 0% of each run, Pallas kernels for 0% -> 0%
where the time goes in v1:
time: 68.1 us; the launch traced here: 67.8 us
  Pallas kernels  59.8 us (88%)
  local copies, waits for them, and re-layouts  7.33 us (11%)
    pallas_call x1, Pallas kernels, fused(): pl.pallas_call(functools.partial(kernel, segs, pens), out_shape=(jax.Shap...  59.8 us
    unnamed x12, local copies, waits for them, and re-layouts  6.71 us

profile of v1, /device:TPU:0, one launch (start us, length us, event | category | flops | bytes accessed | tf_op | source)
XLA Modules:
  0.0 67.8 jit_solution(9077822836417331753)
XLA Ops:
  0.6 0.0 copy-start
  0.6 1.2 %copy-done = bf16[1152,384]{1,0:T(8,128)(2,1)S(1)} copy-done((bf16[1152,384]{1,0:T(8,128)(2,1)S(1)}, bf16[1152,384]{1,0:T(8,128)(2,1)}, u32[]{:S(2)}) %copy-start) | copy-done | bytes 884760
  1.8 0.0 copy-start.1
  1.8 1.1 %copy-done.1 = f32[384,384]{1,0:T(8,128)S(1)} copy-done((f32[384,384]{1,0:T(8,128)S(1)}, f32[384,384]{1,0:T(8,128)}, u32[]{:S(2)}) %copy-start.1) | copy-done | bytes 589848
  2.9 0.0 copy-start.2
  2.9 1.1 %copy-done.2 = f32[384,384]{1,0:T(8,128)S(1)} copy-done((f32[384,384]{1,0:T(8,128)S(1)}, f32[384,384]{1,0:T(8,128)}, u32[]{:S(2)}) %copy-start.2) | copy-done | bytes 589848
  3.9 0.0 copy-start.3
  3.9 1.0 %copy-done.3 = bf16[2,192,576]{2,1,0:T(8,128)(2,1)S(1)} copy-done((bf16[2,192,576]{2,1,0:T(8,128)(2,1)S(1)}, bf16[2,192,576]{2,1,0:T(8,128)(2,1)}, u32[]{:S(2)}) %copy-start.3) | copy-done | bytes 442392
  5.0 0.0 copy-start.4
  5.0 1.0 %copy-done.4 = f32[4,48,384]{2,1,0:T(8,128)S(1)} copy-done((f32[4,48,384]{2,1,0:T(8,128)S(1)}, f32[4,48,384]{2,1,0:T(8,128)}, u32[]{:S(2)}) %copy-start.4) | copy-done | bytes 294936
  5.9 59.8 %shard_map.103 = (f32[4,48,384]{2,1,0:T(8,128)S(1)}, f32[4,48,384]{2,1,0:T(8,128)S(1)}, f32[24,128]{1,0:T(8,128)S(1)}) custom-call(f32[4,48,384]{2,1,0:T(8,128)S(1)} %copy-done.4, f32[16,4,48,384]{3,2,1,0:T(8,128)} %krylov_hbm.1, bf16[2,384,576]{2,1,0:T(8,128)(2,1)} %constant.12.clone.into_hbm, bf16[2,192,576]{2,1,0:T(8,128)(2,1)S(1)} %copy-done.3, ...), custom_call_target="tpu_custom_call" | custom-call | tf_op jit(solution)/shard_map/pallas_call | solution.py:490
  65.7 0.6 slice_reduce_fusion
  66.4 0.7 %copy.13 = f32[4,48,384]{2,1,0:T(8,128)} copy(f32[4,48,384]{2,1,0:T(8,128)S(1)} %get-tuple-element.12) | data formatting | bytes 589824
  67.1 0.7 %copy.14 = f32[4,48,384]{2,1,0:T(8,128)} copy(f32[4,48,384]{2,1,0:T(8,128)S(1)} %get-tuple-element.13) | data formatting | bytes 589824
Async XLA Ops:
  0.6 1.2 %copy-start = (bf16[1152,384]{1,0:T(8,128)(2,1)S(1)}, bf16[1152,384]{1,0:T(8,128)(2,1)}, u32[]{:S(2)}) copy-start(bf16[1152,384]{1,0:T(8,128)(2,1)} %constant.14.clone.cas_hbm) | copy-start | bytes 2654212
  1.8 1.1 %copy-start.1 = (f32[384,384]{1,0:T(8,128)S(1)}, f32[384,384]{1,0:T(8,128)}, u32[]{:S(2)}) copy-start(f32[384,384]{1,0:T(8,128)} %constant.17.clone.damping_hbm) | copy-start | bytes 1769476
  2.9 1.1 %copy-start.2 = (f32[384,384]{1,0:T(8,128)S(1)}, f32[384,384]{1,0:T(8,128)}, u32[]{:S(2)}) copy-start(f32[384,384]{1,0:T(8,128)} %constant.16.clone.inverse_hbm) | copy-start | bytes 1769476
  3.9 1.0 %copy-start.3 = (bf16[2,192,576]{2,1,0:T(8,128)(2,1)S(1)}, bf16[2,192,576]{2,1,0:T(8,128)(2,1)}, u32[]{:S(2)}) copy-start(bf16[2,192,576]{2,1,0:T(8,128)(2,1)} %constant.13.clone.back_hbm) | copy-start | bytes 1327108
  5.0 1.0 %copy-start.4 = (f32[4,48,384]{2,1,0:T(8,128)S(1)}, f32[4,48,384]{2,1,0:T(8,128)}, u32[]{:S(2)}) copy-start(f32[4,48,384]{2,1,0:T(8,128)} %state_hbm.1) | copy-start | bytes 884740

commit v2 on v1

--- a/solution.py
+++ b/solution.py
@@ -172,7 +172,7 @@
     state_hbm, krylov_hbm, into_hbm, back_hbm, cas_hbm, slope_hbm, inverse_hbm, damping_hbm,
     residual_ref, next_ref, hess_ref,
     stored, start, into_t, back_t, cas_t, slope_t, inverse, damping,
-    field, wide, tall, base, tangent, mine, theirs, ending, arrived, image,
+    field, wide, tall, bases, tangent, mine, theirs, ending, arrived, image,
     accum, pay, gather_pen, gather_seg, spread, pay_n, norm_pen, norm_seg,
     load_sem, local_sem, in_send, in_recv, fwd_send, swap_send, swap_recv,
     out_send, out_recv, pen_send, pen_recv, seg_send, seg_recv,
@@ -325,11 +325,13 @@
         swap(f, step).start()
 
     def base_step(step):
+        base = bases.at[step]
         derive(0, base)
         upper, lower = slice(0, half), slice(half, modes_z)
         give_back(0, step, base[0, upper] * base[1, lower] - base[1, upper] * base[0, lower])
 
     def tangent_step(step):
+        base = bases.at[step]
         derive(1, tangent)
         upper, lower = slice(0, half), slice(half, modes_z)
         give_back(
@@ -369,19 +371,20 @@
         load.wait()
     complete(0)
     base_step(0)
-    relay(1)
-    complete(1)
-    tangent_step(0)
     loads[5].wait()
-    for f in range(2):
-        for copy in forwards[f]:
-            copy.wait_send()
+    for copy in forwards[0]:
+        copy.wait_send()
     for step in range(1, STEPS):
         update(0, step - 1)
         base_step(step)
+    relay(1)
+    finish(0)
+    complete(1)
+    tangent_step(0)
+    for copy in forwards[1]:
+        copy.wait_send()
+    for step in range(1, STEPS):
         update(1, step - 1)
-        if step == STEPS - 1:
-            finish(0)
         tangent_step(step)
     finish(1)
     loads[6].wait()
@@ -494,7 +497,7 @@
             jax.ShapeDtypeStruct(state.shape, f32),
             jax.ShapeDtypeStruct((kry + 8, 128), f32),
         ),
-        in_specs=[pl.BlockSpec(memory_space=pl.ANY)] * 8,
+        in_specs=[pl.BlockSpec(memory_space=pltpu.HBM)] * 8,
         out_specs=(pl.BlockSpec(memory_space=pltpu.VMEM),) * 3,
         scratch_shapes=[
             vmem(krylov.shape, f32),
@@ -508,7 +511,7 @@
             vmem((2, modes_z, modes_x), f32),
             vmem((3 * half, 2 * modes_x), bf16),
             vmem((modes_z, 3 * modes_x), bf16),
-            vmem((2, modes_z, modes_x), f32),
+            vmem((STEPS, 2, modes_z, modes_x), f32),
             vmem((2, modes_z, modes_x), f32),
             vmem((2 * STEPS, half, modes_x), f32),
             vmem((2 * STEPS, half, modes_x), f32),
@@ -538,7 +541,7 @@
             dma((2, segs)),
         ],
         compiler_params=pltpu.CompilerParams(
-            collective_id=0, has_side_effects=True, vmem_limit_bytes=50 * 1024 * 1024
+            collective_id=0, has_side_effects=True, vmem_limit_bytes=63_400_000
         ),
     )(state, krylov, *[jnp.asarray(t) for t in tables_of])
     return residual, next_vector, hess[:kry + 1, 0]

time: 68.1 us -> 64.5 us (0.947)
  local copies, waits for them, and re-layouts: 7.33 us -> 4.72 us
  Pallas kernels: 59.8 us -> 59 us
    unnamed x12 -> x2, local copies, waits for them, and re-layouts: 6.71 us -> 3.39 us
    pallas_call x1, Pallas kernels: 59.8 us -> 59 us  [fused(): pl.pallas_call(functools.partial(kernel, segs, pens), out_shape=(jax.Shap...]
    slice x1, local copies, waits for them, and re-layouts: 0.63 us -> 1.33 us  [fused(): return (residual, next_vector, hess[:kry + 1, 0])]
where the time goes in v2:
time: 64.5 us; the launch traced here: 64.3 us
  Pallas kernels  59 us (91%)
  local copies, waits for them, and re-layouts  4.72 us (7%)
    pallas_call x1, Pallas kernels, fused(): pl.pallas_call(functools.partial(kernel, segs, pens), out_shape=(jax.Shap...  59 us
    unnamed x2, local copies, waits for them, and re-layouts  3.39 us
    slice x1, local copies, waits for them, and re-layouts, fused(): return (residual, next_vector, hess[:kry + 1, 0])  1.33 us

profile of v2, /device:TPU:0, one launch (start us, length us, event | category | flops | bytes accessed | tf_op | source)
XLA Modules:
  0.0 64.3 jit_solution(5653610742819635039)
XLA Ops:
  0.6 59.0 %shard_map.103 = (f32[4,48,384]{2,1,0:T(8,128)}, f32[4,48,384]{2,1,0:T(8,128)}, f32[24,128]{1,0:T(8,128)}) custom-call(f32[4,48,384]{2,1,0:T(8,128)} %state_hbm.1, f32[16,4,48,384]{3,2,1,0:T(8,128)} %krylov_hbm.1, bf16[2,384,576]{2,1,0:T(8,128)(2,1)} %constant.12.clone.into_hbm, bf16[2,192,576]{2,1,0:T(8,128)(2,1)} %constant.13.clone.back_hbm, ...), custom_call_target="tpu_custom_call" | custom-call | tf_op jit(solution)/shard_map/pallas_call | solution.py:493
  59.6 1.3 %slice_reduce_fusion = f32[17]{0:T(128)} fusion(f32[24,128]{1,0:T(8,128)} %get-tuple-element.8), kind=kLoop, calls=%fused_computation | loop fusion | bytes 136 | tf_op jit(solution)/shard_map/slice | solution.py:547
  60.9 1.7 %copy.13 = f32[4,48,384]{2,1,0:T(8,128)} copy(f32[4,48,384]{2,1,0:T(8,128)} %get-tuple-element.12) | data formatting | bytes 589824
  62.6 1.7 %copy.14 = f32[4,48,384]{2,1,0:T(8,128)} copy(f32[4,48,384]{2,1,0:T(8,128)} %get-tuple-element.13) | data formatting | bytes 589824
